TPU v7x, 32 devices: a whole 2x2x4 slice. The times are simulated.
32 devices in a mesh: band: 4 (over z), dom: 8 (over y, x, core).
Axes of the slice: x: 2, y: 2, z: 4, core: 2. Of those that a mesh axis runs over, the one named last changes fastest.
Arguments:
- orbitals: float32 [128, 32, 12288], P('band', 'dom'), may hold values from -8 to 8
- potential: float32 [32, 12288], P('dom'), may hold values from -2 to 2
Outputs:
- updated: float32 [128, 32, 12288], P('band', 'dom')
All inputs are finite; a program needn't handle non-finite values.
Results may differ from a plain program's by a relative error of at most 0.00012.
Values sent between devices are 32-bit elements; how exact they have to be, the bound alone decides.
A program may use at most 384 MiB of HBM per device.

v0:
```python
import jax
import jax.numpy as jnp
from jax import lax
from jax.sharding import PartitionSpec as P

NZ = 128


COEFFS = (-205.0 / 72.0, 8.0 / 5.0, -1.0 / 5.0, 8.0 / 315.0, -1.0 / 560.0)


def extended(cells, sides, width):
    for axis, dim in sides:
        count = lax.axis_size(axis)
        head = lax.slice_in_dim(cells, 0, width, axis=dim)
        tail = lax.slice_in_dim(cells, cells.shape[dim] - width, cells.shape[dim], axis=dim)
        cells = jnp.concatenate(
            [
                lax.ppermute(tail, axis, [(i, (i + 1) % count) for i in range(count)]),
                cells,
                lax.ppermute(head, axis, [((i + 1) % count, i) for i in range(count)]),
            ],
            axis=dim,
        )
    return cells


def from_root(block, axis, holder):
    block = jnp.where(lax.axis_index(axis) == holder, block, jnp.zeros_like(block))
    return lax.psum(block, axis)


def plane_laplacian(orbital, row_len):
    depth_index = lax.broadcasted_iota(jnp.int32, orbital.shape, orbital.ndim - 1) % row_len
    total = 2.0 * COEFFS[0] * orbital
    for offset in range(1, 5):
        beside_y = jnp.roll(orbital, offset * row_len, -1) + jnp.roll(
            orbital, -offset * row_len, -1
        )
        below_z = jnp.where(
            depth_index >= offset,
            jnp.roll(orbital, offset, -1),
            jnp.roll(orbital, offset - row_len, -1),
        )
        above_z = jnp.where(
            depth_index < row_len - offset,
            jnp.roll(orbital, -offset, -1),
            jnp.roll(orbital, row_len - offset, -1),
        )
        total = total + COEFFS[offset] * (beside_y + below_z + above_z)
    return total


def products(left, right):
    return jnp.dot(left, right.T, precision=lax.Precision.HIGHEST)


def body(orbitals, potential):
    planes = orbitals.shape[1]
    padded = extended(orbitals, (("dom", 1),), 4)
    along_x = COEFFS[0] * orbitals
    for offset in range(1, 5):
        along_x = along_x + COEFFS[offset] * (
            padded[:, 4 + offset : 4 + offset + planes]
            + padded[:, 4 - offset : 4 - offset + planes]
        )
    applied = -0.5 * (plane_laplacian(orbitals, NZ) + along_x) + potential[None] * orbitals
    own_rows = applied.reshape(applied.shape[0], -1)
    cell_count = planes * orbitals.shape[2] * lax.axis_size("dom")
    is_first = lax.axis_index("band") == 0
    correlation = lax.psum(products(own_rows, own_rows), "dom") / cell_count
    lower_tri = jnp.linalg.cholesky(correlation)
    basis_rows = jax.scipy.linalg.solve_triangular(lower_tri, own_rows, lower=True)
    block_rows = from_root(basis_rows, "band", 0)
    coeffs = lax.psum(products(block_rows, own_rows), "dom") / cell_count
    projected = own_rows - jnp.dot(coeffs.T, block_rows, precision=lax.Precision.HIGHEST)
    result = jnp.where(is_first, block_rows, projected)
    return result.reshape(orbitals.shape)


def solution(mesh):
    placed = (P("band", "dom", None), P("dom", None))
    return jax.shard_map(
        body, mesh=mesh, in_specs=placed, out_specs=P("band", "dom", None), check_vma=False
    )
```

profile of v0, /device:TPU:0, one launch (start us, length us, event | category | flops | bytes accessed | tf_op | source)
XLA Modules:
  0.0 643.2 jit_solution(14980378327920977012)
XLA Ops:
  6.5 0.0 all-reduce.2.cloned.1.call-start
  6.5 3.3 collective-permute-start
  9.9 0.0 collective-permute-start.1
  9.9 12.6 %fusion.50 = (f32[32,4,12287]{2,1,0:T(4,128)}, f32[32,4,12287]{2,1,0:T(4,128)}) fusion(f32[32,4,12288]{2,1,0:T(4,128)} %param.2), kind=kLoop, calls=%fused_computation.89 | loop fusion | bytes 25163776 | tf_op jit(solution)/shard_map/jit(_roll_static)/slice | solution.py:42
  22.5 12.6 %fusion.51 = (f32[32,4,12161]{2,1,0:T(4,128)}, f32[32,4,12161]{2,1,0:T(4,128)}) fusion(f32[32,4,12288]{2,1,0:T(4,128)} %param.2), kind=kLoop, calls=%fused_computation.90 | loop fusion | bytes 24905728 | tf_op jit(solution)/shard_map/jit(_roll_static)/slice | solution.py:43
  35.1 12.5 %fusion.56 = (f32[32,4,12286]{2,1,0:T(4,128)}, f32[32,4,12286]{2,1,0:T(4,128)}) fusion(f32[32,4,12288]{2,1,0:T(4,128)} %param.2), kind=kLoop, calls=%fused_computation.95 | loop fusion | bytes 25161728 | tf_op jit(solution)/shard_map/jit(_roll_static)/slice | solution.py:42
  47.6 12.7 %fusion.57 = (f32[32,4,12162]{2,1,0:T(4,128)}, f32[32,4,12162]{2,1,0:T(4,128)}) fusion(f32[32,4,12288]{2,1,0:T(4,128)} %param.2), kind=kLoop, calls=%fused_computation.96 | loop fusion | bytes 24907776 | tf_op jit(solution)/shard_map/jit(_roll_static)/slice | solution.py:43
  60.3 12.5 %fusion.62 = (f32[32,4,12285]{2,1,0:T(4,128)}, f32[32,4,12285]{2,1,0:T(4,128)}) fusion(f32[32,4,12288]{2,1,0:T(4,128)} %param.2), kind=kLoop, calls=%fused_computation.101 | loop fusion | bytes 25159680 | tf_op jit(solution)/shard_map/jit(_roll_static)/slice | solution.py:42
  72.8 12.6 %fusion.63 = (f32[32,4,12163]{2,1,0:T(4,128)}, f32[32,4,12163]{2,1,0:T(4,128)}) fusion(f32[32,4,12288]{2,1,0:T(4,128)} %param.2), kind=kLoop, calls=%fused_computation.102 | loop fusion | bytes 24909824 | tf_op jit(solution)/shard_map/jit(_roll_static)/slice | solution.py:43
  85.4 12.9 %fusion.68 = (f32[32,4,12284]{2,1,0:T(4,128)}, f32[32,4,12284]{2,1,0:T(4,128)}) fusion(f32[32,4,12288]{2,1,0:T(4,128)} %param.2), kind=kLoop, calls=%fused_computation.107 | loop fusion | bytes 25157632 | tf_op jit(solution)/shard_map/jit(_roll_static)/slice | solution.py:42
  98.3 12.7 %fusion.69 = (f32[32,4,12164]{2,1,0:T(4,128)}, f32[32,4,12164]{2,1,0:T(4,128)}) fusion(f32[32,4,12288]{2,1,0:T(4,128)} %param.2), kind=kLoop, calls=%fused_computation.108 | loop fusion | bytes 24911872 | tf_op jit(solution)/shard_map/jit(_roll_static)/slice | solution.py:43
  111.0 9.9 %fusion.48 = (f32[32,4,12160]{2,1,0:T(4,128)}, f32[32,4,12160]{2,1,0:T(4,128)}) fusion(f32[32,4,12288]{2,1,0:T(4,128)} %param.2), kind=kLoop, calls=%fused_computation.87 | loop fusion | bytes 24903680 | tf_op jit(solution)/shard_map/jit(_roll_static)/slice | solution.py:37
  120.9 9.8 %fusion.54 = (f32[32,4,12032]{2,1,0:T(4,128)}, f32[32,4,12032]{2,1,0:T(4,128)}) fusion(f32[32,4,12288]{2,1,0:T(4,128)} %param.2), kind=kLoop, calls=%fused_computation.93 | loop fusion | bytes 24641536 | tf_op jit(solution)/shard_map/jit(_roll_static)/slice | solution.py:37
  130.6 1.1 fusion.65
  131.7 1.1 fusion.59
  132.8 1.0 fusion.53
  133.8 1.0 fusion.49
  134.8 1.0 fusion.52
  135.7 1.0 fusion.55
  136.7 1.0 fusion.58
  137.7 1.0 fusion.61
  138.7 1.0 fusion.64
  139.6 1.0 fusion.67
  140.6 0.9 fusion.47
  141.5 1.0 fusion.70
  142.5 9.7 %fusion.60 = (f32[32,4,11904]{2,1,0:T(4,128)}, f32[32,4,11904]{2,1,0:T(4,128)}) fusion(f32[32,4,12288]{2,1,0:T(4,128)} %param.2), kind=kLoop, calls=%fused_computation.99 | loop fusion | bytes 24379392 | tf_op jit(solution)/shard_map/jit(_roll_static)/slice | solution.py:37
  152.2 9.8 %fusion.66 = (f32[32,4,11776]{2,1,0:T(4,128)}, f32[32,4,11776]{2,1,0:T(4,128)}) fusion(f32[32,4,12288]{2,1,0:T(4,128)} %param.2), kind=kLoop, calls=%fused_computation.105 | loop fusion | bytes 24117248 | tf_op jit(solution)/shard_map/jit(_roll_static)/slice | solution.py:37
  162.0 0.0 collective-permute-done
  162.0 0.0 collective-permute-done.1
  162.0 0.0 copy-done.1
  162.0 135.8 %multiply_add_fusion = f32[32,4,12288]{2,1,0:T(4,128)} fusion(f32[32,4,12288]{2,1,0:T(4,128)} %param.2, f32[32,4,12288]{2,1,0:T(4,128)} %collective-permute-done.1, f32[32,4,12288]{2,1,0:T(4,128)} %collective-permute-done, f32[32,4,12164]{2,1,0:T(4,128)} %get-tuple-element.50, f32[32,4,124]{2,1,0:T(4,128)S(1)} %get-tuple-element.52, ...), kind=kLoop, calls=%fused_computation.66 | loop fusion | flops 133693440 | bytes 176467968 | tf_op jit(solution)/shard_map/add | solution.py:67
  297.8 15.8 %fusion.34 = f32[32,32]{0,1:T(8,128)S(1)} fusion(f32[32,4,12288]{2,1,0:T(4,128)} %multiply_add_fusion), kind=kOutput, calls=%fused_computation.67 | convolution fusion | flops 603979776 | bytes 6295552 | tf_op jit(solution)/shard_map/dot_general | solution.py:55
  313.6 25.1 %psum.21 = f32[32,32]{0,1:T(8,128)S(1)} all-reduce(f32[32,32]{0,1:T(8,128)S(1)} %fusion.34), channel_id=1, replica_groups=mesh['band'=4,'dom'=8] {'dom'}, use_global_device_ids=true, to_apply=%region_0.1 | all-reduce | flops 1024 | bytes 8192 | tf_op jit(solution)/shard_map/psum | solution.py:71
  338.7 0.1 copy.6
  338.8 2.9 cholesky.16
  341.8 0.6 compare_reduce_fusion
  342.4 0.7 fusion.41
  343.1 2.4 custom-call.7
  345.5 6.5 %copy.9 = f32[4,8,4,12288]{3,1,2,0:T(8,128)S(1)} copy(f32[4,8,4,12288]{3,2,1,0:T(4,128)} %bitcast.20) | data formatting | bytes 12582912
  352.0 0.0 copy-start
  352.0 2.6 copy-done
  354.6 7.2 %convolution_select_fusion = f32[32,49152]{1,0:T(8,128)} fusion(f32[32,49152]{1,0:T(8,128)S(1)} %bitcast.17, pred[]{:T(512)S(6)} %eq.6, f32[1,32,32]{1,2,0:T(8,128)S(1)} %custom-call.7), kind=kOutput, calls=%fused_computation.2 | convolution fusion | flops 605552640 | bytes 12587009 | tf_op jit(solution)/shard_map/jit(_solve_triangular)/triangular_solve | solution.py:73
  361.8 0.0 all-reduce.2.cloned.1.call-update
  361.9 222.4 %all-reduce.2.cloned.1.call-done = f32[32,49152]{1,0:T(8,128)} async-done(((f32[32,49152]{1,0:T(8,128)}), f32[32,49152]{1,0:T(8,128)}) %all-reduce.2.cloned.1.call-update) | async-done | bytes 6291472 | tf_op jit(solution)/shard_map/psum | solution.py:30
  584.2 8.2 %fusion.71 = f32[32,32]{0,1:T(8,128)S(1)} fusion(f32[32,49152]{1,0:T(8,128)} %all-reduce.2.cloned.1.call-done, f32[32,49152]{1,0:T(8,128)} %bitcast.18), kind=kOutput, calls=%fused_computation.110 | convolution fusion | flops 603979776 | bytes 12587008 | tf_op jit(solution)/shard_map/dot_general | solution.py:55
  592.5 24.3 %psum.23 = f32[32,32]{0,1:T(8,128)S(1)} all-reduce(f32[32,32]{0,1:T(8,128)S(1)} %fusion.71), channel_id=1, replica_groups=mesh['band'=4,'dom'=8] {'dom'}, use_global_device_ids=true, to_apply=%region_4.5 | all-reduce | flops 1024 | bytes 8192 | tf_op jit(solution)/shard_map/psum | solution.py:75
  616.8 11.2 %fusion = f32[32,49152]{1,0:T(8,128)} fusion(f32[32,49152]{1,0:T(8,128)} %all-reduce.2.cloned.1.call-done, f32[32,49152]{1,0:T(8,128)} %bitcast.19, pred[]{:T(512)S(6)} %eq.6, f32[32,32]{0,1:T(8,128)S(1)} %psum.23), kind=kOutput, calls=%fused_computation.1 | convolution fusion | flops 607126528 | bytes 18878464 | tf_op jit(solution)/shard_map/dot_general | solution.py:76
  628.0 7.9 %reshape.18 = f32[32,4,12288]{2,1,0:T(4,128)} reshape(f32[32,49152]{1,0:T(8,128)} %fusion) | data formatting | bytes 12582912 | tf_op jit(solution)/shard_map/reshape | solution.py:78
  (6 shorter events, 0.1 us)
Async XLA Ops:
  6.5 577.7 %all-reduce.2.cloned.1.call-start = ((), (), s32[]{:S(2)}) async-start(), calls=%async_computation | async-start | bytes 12582912 | tf_op jit(solution)/shard_map/psum | solution.py:30
  6.5 155.5 %collective-permute-start = (f32[32,4,12288]{2,1,0:T(4,128)}, f32[32,4,12288]{2,1,0:T(4,128)}, u32[]{:S(2)}, u32[]{:S(2)}) collective-permute-start(f32[32,4,12288]{2,1,0:T(4,128)} %param.2), channel_id=1, source_target_pairs={{1,0},{2,1},{3,2},{4,3},{5,4},{6,5},{7,6},{0,7},{9,8},{10,9},{11,1... | collective-permute-start | bytes 18874376 | tf_op jit(solution)/shard_map/ppermute | solution.py:21
  9.9 152.1 %collective-permute-start.1 = (f32[32,4,12288]{2,1,0:T(4,128)}, f32[32,4,12288]{2,1,0:T(4,128)}, u32[]{:S(2)}, u32[]{:S(2)}) collective-permute-start(f32[32,4,12288]{2,1,0:T(4,128)} %param.2), channel_id=1, source_target_pairs={{0,1},{1,2},{2,3},{3,4},{4,5},{5,6},{6,7},{7,0},{8,9},{9,10},{10,1... | collective-permute-start | bytes 18874376 | tf_op jit(solution)/shard_map/ppermute | solution.py:19
  152.2 9.8 %copy-start.1 = (f32[4,12288]{1,0:T(4,128)S(1)}, f32[4,12288]{1,0:T(4,128)}, u32[]{:S(2)}) copy-start(f32[4,12288]{1,0:T(4,128)} %param.3) | copy-start | bytes 589828
  352.0 2.6 copy-start
Sparse Core Ops, SparseCore 0:
  362.0 222.1 all-reduce.1
where the time goes:
time: 653 us; the launch traced here: 643 us
  waiting for transfers between devices  222 us (34%)
  local copies, waits for them, and re-layouts  169 us (26%)
  other arithmetic  143 us (22%)
  blocking collectives  49.5 us (8%)
  matrix products  42.5 us (7%)
  between operations  14 us (2%)
    psum x1, waiting for transfers between devices, from_root(): return lax.psum(block, axis)  222 us
    add x1, other arithmetic, body(): -0.5 * (plane_laplacian(orbitals, NZ) + along_x)  136 us
    slice x8, local copies, waits for them, and re-layouts, plane_laplacian(): jnp.roll(orbital, offset - row_len, -1)  54.5 us
    slice x8, local copies, waits for them, and re-layouts, plane_laplacian(): jnp.roll(orbital, offset, -1)  54.4 us
    slice x8, local copies, waits for them, and re-layouts, plane_laplacian(): jnp.roll(orbital, offset * row_len, -1)  43.1 us
    psum x1, blocking collectives, body(): correlation = lax.psum(products(own_rows, own_rows), 'dom') / cell_count  25.1 us
    psum x1, blocking collectives, body(): coeffs = lax.psum(products(block_rows, own_rows), 'dom') / cell_count  24.3 us
    dot_general x2, matrix products, products(): return jnp.dot(left, right.T, precision=lax.Precision.HIGHEST)  24 us
  transfers between devices with their start and end apart: 3, of which 1 were waited for; matrix products, arithmetic and copies ran while one was open for 24% of the time, Pallas kernels for 0%

commit v1 on v0

v1 whole, which is shorter than its diff:
```python
import functools

import jax
import jax.numpy as jnp
from jax import lax
from jax.experimental import pallas as pl
from jax.experimental.pallas import tpu as pltpu
from jax.sharding import PartitionSpec as P

NZ = 128
WIDTH = 4
COEFFS = (-205.0 / 72.0, 8.0 / 5.0, -1.0 / 5.0, 8.0 / 315.0, -1.0 / 560.0)
HALF = tuple(-0.5 * c for c in COEFFS)
CHUNK_Y = 4
WINDOW = 4
MIB = 1024 * 1024
NT = (((1,), (1,)), ((), ()))
MESH = pl.DeviceIdType.MESH


def split(value):
    high = value.astype(jnp.bfloat16)
    low = (value - high.astype(jnp.float32)).astype(jnp.bfloat16)
    return high, low


def apply_kernel(
    nb, nd, planes, ny,
    x_ref, v_ref, a_out, b_out, g_out,
    nat, xs, from_left, from_right, own, blk, acc, part, parts,
    load_sem, halo_send, halo_recv, blk_send, blk_recv, a_sem, b_sem, part_send, part_recv, g_sem,
):
    block = xs.shape[1]
    rows = planes * ny
    chunk = planes * CHUNK_Y
    chunks = ny // CHUNK_Y
    band = lax.axis_index("band")
    dom = lax.axis_index("dom")
    right = lax.rem(dom + 1, nd)
    left = lax.rem(dom + nd - 1, nd)

    def load(c):
        span = pl.ds(pl.multiple_of(c * chunk, chunk), chunk)
        return pltpu.make_async_copy(x_ref.at[:, span, :], nat.at[:, span, :], load_sem.at[c])

    def halo(c, way):
        span = pl.ds(c * chunk, chunk)
        return pltpu.make_async_remote_copy(
            src_ref=xs.at[span],
            dst_ref=(from_left, from_right)[way].at[span],
            send_sem=halo_send.at[way, c],
            recv_sem=halo_recv.at[way, c],
            device_id=(band, (right, left)[way]),
            device_id_type=MESH,
        )

    def onward(c):
        span = pl.ds(c * chunk, chunk)
        return pltpu.make_async_remote_copy(
            src_ref=blk.at[span],
            dst_ref=blk.at[span],
            send_sem=blk_send.at[c],
            recv_sem=blk_recv.at[c],
            device_id=(lax.rem(band + 1, nb), dom),
            device_id_type=MESH,
        )

    def save(c, which):
        span = pl.ds(c * chunk, chunk)
        source, target, sem = ((own, a_out, a_sem), (blk, b_out, b_sem))[which]
        return pltpu.make_async_copy(source.at[span], target.at[span], sem.at[c])

    def total_to(step):
        peer = lax.rem(dom + step, nd)
        return pltpu.make_async_remote_copy(
            src_ref=part, dst_ref=parts.at[dom], send_sem=part_send.at[step],
            recv_sem=part_recv.at[dom], device_id=(band, peer), device_id_type=MESH,
        )

    def total_from(step):
        peer = lax.rem(dom + nd - step, nd)
        return pltpu.make_async_remote_copy(
            src_ref=part, dst_ref=parts.at[peer], send_sem=part_send.at[step],
            recv_sem=part_recv.at[peer], device_id=(band, peer), device_id_type=MESH,
        )

    @pl.loop(0, chunks)
    def _(c):
        load(c).start()

    barrier = pltpu.get_barrier_semaphore()
    for step in range(1, nd):
        pl.semaphore_signal(
            barrier, inc=1, device_id=(band, lax.rem(dom + step, nd)), device_id_type=MESH
        )

    for step in (1, nb - 1):
        pl.semaphore_signal(
            barrier, inc=1, device_id=(lax.rem(band + step, nb), dom), device_id_type=MESH
        )
    pl.semaphore_wait(barrier, nd + 1)

    acc[...] = jnp.zeros_like(acc)
    flat = nat.reshape(block * rows, NZ)

    @pl.loop(0, chunks)
    def _(c):
        load(c).wait()

        @pl.loop(0, chunk)
        def _(i):
            row = c * chunk + i
            xs[row] = flat[pl.ds(row, block, stride=rows), :]

        @pl.when(c < WINDOW)
        def _():
            halo(c, 0).start()
            halo(c, 1).start()

    def hamiltonian(c):
        @pl.loop(0, CHUNK_Y)
        def _(i):
            y = c * CHUNK_Y + i
            base = y * planes
            before = [lax.rem(y + ny - k, ny) * planes for k in range(WIDTH + 1)]
            after = [lax.rem(y + k, ny) * planes for k in range(WIDTH + 1)]

            def plane(p):
                if p < 0:
                    return from_left[base + planes + p]
                if p >= planes:
                    return from_right[base + p - planes]
                return xs[base + p]

            for p in range(planes):
                centre = xs[base + p]
                total = (v_ref[pl.ds(base + p, 1), :] + 3.0 * HALF[0]) * centre
                for k in range(1, WIDTH + 1):
                    near = (
                        (plane(p - k) + plane(p + k))
                        + (xs[before[k] + p] + xs[after[k] + p])
                        + (pltpu.roll(centre, k, 1) + pltpu.roll(centre, NZ - k, 1))
                    )
                    total = total + HALF[k] * near
                own[base + p] = total

                @pl.when(band == 0)
                def _():
                    blk[base + p] = total

    def gram(c):
        @pl.loop(0, CHUNK_Y)
        def _(i):
            base = (c * CHUNK_Y + i) * planes
            both = jnp.concatenate(
                [
                    jnp.concatenate([blk[base + p] for p in range(planes)], axis=1),
                    jnp.concatenate([own[base + p] for p in range(planes)], axis=1),
                ],
                axis=0,
            )
            high, low = split(both)
            lhs = jnp.concatenate([high, low], axis=0)
            rhs = jnp.concatenate([high[:block], low[:block]], axis=0)
            acc[...] += lax.dot_general(lhs, rhs, NT, preferred_element_type=jnp.float32)

    @pl.loop(0, chunks + nb - 1)
    def _(step):
        @pl.when(step < chunks)
        def _():
            @pl.when(step + WINDOW < chunks)
            def _():
                halo(step + WINDOW, 0).start()
                halo(step + WINDOW, 1).start()

            halo(step, 0).wait_recv()
            halo(step, 1).wait_recv()
            hamiltonian(step)

        c = step - band

        @pl.when(jnp.logical_and(c >= 0, c < chunks))
        def _():
            @pl.when(band > 0)
            def _():
                onward(c).wait_recv()

            @pl.when(band < nb - 1)
            def _():
                onward(c).start()

            save(c, 0).start()
            save(c, 1).start()
            gram(c)

    found = acc[...]
    found = found[: 2 * block] + found[2 * block :]
    found = found[:, :block] + found[:, block:]
    found = jnp.concatenate([found, jnp.zeros((2 * block, NZ - block), jnp.float32)], axis=1)
    part[...] = found
    for step in range(1, nd):
        total_to(step).start()
    parts[dom] = found
    for step in range(1, nd):
        total_from(step).wait_recv()
    summed = parts[0]
    for step in range(1, nd):
        summed = summed + parts[step]
    part_sum = summed

    @pl.loop(0, chunks)
    def _(c):
        halo(c, 0).wait_send()
        halo(c, 1).wait_send()
        save(c, 0).wait()
        save(c, 1).wait()

        @pl.when(band < nb - 1)
        def _():
            onward(c).wait_send()

    for step in range(1, nd):
        total_to(step).wait_send()
    part[...] = part_sum
    out = pltpu.make_async_copy(part, g_out, g_sem)
    out.start()
    out.wait()


def finish_kernel(count, planes, g_ref, a_ref, b_ref, o_ref, weights):
    block = a_ref.shape[1]
    rows = a_ref.shape[0]
    band = lax.axis_index("band")

    @pl.when(pl.program_id(0) == 0)
    def _():
        gram = g_ref[...] * (1.0 / count)
        corr = gram[:block, :block]
        cross = gram[block:, :block]
        row_id = lax.broadcasted_iota(jnp.int32, (block, block), 0)
        col_id = lax.broadcasted_iota(jnp.int32, (block, block), 1)
        work = jnp.concatenate([corr, jnp.where(row_id == col_id, 1.0, 0.0)], axis=1)
        row_of = lax.broadcasted_iota(jnp.int32, (block, 1), 0)
        for k in range(block):
            scale = 1.0 / jnp.sqrt(work[k : k + 1, k : k + 1])
            pivot = work[k : k + 1, :] * scale
            factor = jnp.where(row_of > k, work[:, k : k + 1] * scale, 0.0)
            work = jnp.where(row_of == k, pivot, work - factor * pivot)
        inverse = jnp.where(col_id <= row_id, work[:, block:], 0.0)
        exact = dict(precision=lax.Precision.HIGHEST, preferred_element_type=jnp.float32)
        coeffs = lax.dot_general(cross, inverse, NT, **exact)
        mixed = jnp.dot(coeffs, inverse, **exact)
        chosen = jnp.where(band == 0, -inverse, mixed)
        high, low = split(chosen)
        weights[...] = jnp.concatenate([high, low, high, low], axis=1)

    keep = jnp.where(band == 0, 0.0, 1.0).astype(jnp.float32)
    lhs = weights[...]
    flat = o_ref.reshape(block * rows, NZ)

    @pl.loop(0, rows // planes)
    def _(i):
        base = i * planes
        high, low = split(jnp.concatenate([b_ref[base + p] for p in range(planes)], axis=1))
        rhs = jnp.concatenate([high, high, low, low], axis=0)
        change = jnp.dot(lhs, rhs, preferred_element_type=jnp.float32)
        for p in range(planes):
            flat[pl.ds(base + p, block, stride=rows), :] = (
                keep * a_ref[base + p] - change[:, p * NZ : (p + 1) * NZ]
            )


def body(orbitals, potential):
    block, planes, plane = orbitals.shape
    ny = plane // NZ
    rows = planes * ny
    nb, nd = lax.axis_size("band"), lax.axis_size("dom")
    chunk_count = ny // CHUNK_Y
    x = orbitals.reshape(block, planes, ny, NZ).transpose(0, 2, 1, 3).reshape(block, rows, NZ)
    v = potential.reshape(planes, ny, NZ).transpose(1, 0, 2).reshape(rows, NZ)
    cells = jax.ShapeDtypeStruct((rows, block, NZ), jnp.float32)
    cells_vmem = pltpu.VMEM((rows, block, NZ), jnp.float32)
    dma = pltpu.SemaphoreType.DMA
    hbm = pl.BlockSpec(memory_space=pl.ANY)
    applied, basis, gram = pl.pallas_call(
        functools.partial(apply_kernel, nb, nd, planes, ny),
        out_shape=(cells, cells, jax.ShapeDtypeStruct((2 * block, NZ), jnp.float32)),
        in_specs=[hbm, pl.BlockSpec(memory_space=pltpu.VMEM)],
        out_specs=(hbm, hbm, hbm),
        scratch_shapes=[
            pltpu.VMEM((block, rows, NZ), jnp.float32),
            cells_vmem, cells_vmem, cells_vmem, cells_vmem, cells_vmem,
            pltpu.VMEM((4 * block, 2 * block), jnp.float32),
            pltpu.VMEM((2 * block, NZ), jnp.float32),
            pltpu.VMEM((nd, 2 * block, NZ), jnp.float32),
            dma((chunk_count,)), dma((2, chunk_count)), dma((2, chunk_count)),
            dma((chunk_count,)), dma((chunk_count,)), dma((chunk_count,)), dma((chunk_count,)),
            dma((nd,)), dma((nd,)), dma,
        ],
        compiler_params=pltpu.CompilerParams(
            collective_id=0, has_side_effects=True, vmem_limit_bytes=48 * MIB
        ),
        cost_estimate=pl.CostEstimate(
            flops=80 * block * rows * NZ, bytes_accessed=12 * block * rows * NZ, transcendentals=0
        ),
        name="apply_and_share",
    )(x, v)
    step_rows = 8 * planes
    count = rows * NZ * nd
    cell_spec = pl.BlockSpec((step_rows, block, NZ), lambda i: (i, 0, 0))
    result = pl.pallas_call(
        functools.partial(finish_kernel, count, planes),
        grid=(rows // step_rows,),
        out_shape=jax.ShapeDtypeStruct((block, rows, NZ), jnp.float32),
        in_specs=[pl.BlockSpec((2 * block, NZ), lambda i: (0, 0)), cell_spec, cell_spec],
        out_specs=pl.BlockSpec((block, step_rows, NZ), lambda i: (0, i, 0)),
        scratch_shapes=[pltpu.VMEM((block, 4 * block), jnp.bfloat16)],
        compiler_params=pltpu.CompilerParams(vmem_limit_bytes=56 * MIB),
        cost_estimate=pl.CostEstimate(
            flops=80 * block * rows * NZ, bytes_accessed=12 * block * rows * NZ, transcendentals=0
        ),
        name="finish",
    )(gram, applied, basis)
    result = result.reshape(block, ny, planes, NZ).transpose(0, 2, 1, 3)
    return result.reshape(block, planes, plane)


def solution(mesh):
    placed = (P("band", "dom", None), P("dom", None))
    return jax.shard_map(
        body, mesh=mesh, in_specs=placed, out_specs=P("band", "dom", None), check_vma=False
    )
```

time: 653 us -> 197 us (0.30)
  the two profiles are of different devices: /device:TPU:0 before, /device:TPU:31 now
where the time goes in v1:
time: 197 us; the launch traced here: 196 us
  Pallas kernels  194 us (98%)
    pallas_call x1, Pallas kernels, body(): pl.pallas_call(functools.partial(apply_kernel, nb, nd, planes, ny), out_s...  171 us
    pallas_call x1, Pallas kernels, body(): pl.pallas_call(functools.partial(finish_kernel, count, planes), grid=(row...  22.6 us

profile of v1, /device:TPU:31, one launch (start us, length us, event | category | flops | bytes accessed | tf_op | source)
XLA Modules:
  0.0 195.6 jit_solution(4865430281139793658)
XLA Ops:
  0.0 0.0 copy-start
  0.0 0.9 copy-done
  0.9 171.4 %apply_and_share.1 = (f32[384,32,128]{2,1,0:T(8,128)}, f32[384,32,128]{2,1,0:T(8,128)}, f32[64,128]{1,0:T(8,128)S(1)}) custom-call(f32[32,384,128]{2,1,0:T(8,128)} %bitcast.16, f32[384,128]{1,0:T(8,128)S(1)} %bitcast.15), custom_call_target="tpu_custom_call" | custom-call | flops 125829120 | bytes 18874368 | tf_op jit(solution)/shard_map/apply_and_share/pallas_call | solution.py:285
  172.4 0.0 copy-start.1
  172.4 0.6 copy-done.1
  173.0 22.6 %finish.1 = f32[32,384,128]{2,1,0:T(8,128)} custom-call(f32[64,128]{1,0:T(8,128)} %copy-done.1, f32[384,32,128]{2,1,0:T(8,128)} %get-tuple-element.9.a_ref, f32[384,32,128]{2,1,0:T(8,128)} %get-tuple-element.10.b_ref), custom_call_target="tpu_custom_call" | custom-call | flops 125829120 | bytes 18874368 | tf_op jit(solution)/shard_map/finish/pallas_call | solution.py:311
Async XLA Ops:
  0.0 0.9 copy-start
  172.4 0.6 copy-start.1

commit v2 on v1

--- a/solution.py
+++ b/solution.py
@@ -11,8 +11,8 @@
 WIDTH = 4
 COEFFS = (-205.0 / 72.0, 8.0 / 5.0, -1.0 / 5.0, 8.0 / 315.0, -1.0 / 560.0)
 HALF = tuple(-0.5 * c for c in COEFFS)
-CHUNK_Y = 4
-WINDOW = 4
+CHUNK_Y = 2
+WINDOW = 8
 MIB = 1024 * 1024
 NT = (((1,), (1,)), ((), ()))
 MESH = pl.DeviceIdType.MESH
@@ -26,9 +26,9 @@
 
 def apply_kernel(
     nb, nd, planes, ny,
-    x_ref, v_ref, a_out, b_out, g_out,
-    nat, xs, from_left, from_right, own, blk, acc, part, parts,
-    load_sem, halo_send, halo_recv, blk_send, blk_recv, a_sem, b_sem, part_send, part_recv, g_sem,
+    x_ref, v_hbm, a_out, b_out, g_out,
+    nat, xs, from_left, from_right, own, blk, v_ref, acc, part, parts,
+    load_sem, halo_send, halo_recv, blk_send, blk_recv, a_sem, b_sem, part_send, part_recv, g_sem, v_sem,
 ):
     block = xs.shape[1]
     rows = planes * ny
@@ -88,6 +88,9 @@
     def _(c):
         load(c).start()
 
+    potential = pltpu.make_async_copy(v_hbm, v_ref, v_sem)
+    potential.start()
+
     barrier = pltpu.get_barrier_semaphore()
     for step in range(1, nd):
         pl.semaphore_signal(
@@ -116,6 +119,8 @@
         def _():
             halo(c, 0).start()
             halo(c, 1).start()
+
+    potential.wait()
 
     def hamiltonian(c):
         @pl.loop(0, CHUNK_Y)
@@ -242,11 +247,12 @@
         work = jnp.concatenate([corr, jnp.where(row_id == col_id, 1.0, 0.0)], axis=1)
         row_of = lax.broadcasted_iota(jnp.int32, (block, 1), 0)
         for k in range(block):
-            scale = 1.0 / jnp.sqrt(work[k : k + 1, k : k + 1])
-            pivot = work[k : k + 1, :] * scale
-            factor = jnp.where(row_of > k, work[:, k : k + 1] * scale, 0.0)
-            work = jnp.where(row_of == k, pivot, work - factor * pivot)
-        inverse = jnp.where(col_id <= row_id, work[:, block:], 0.0)
+            pivot = work[k : k + 1, :]
+            factor = jnp.where(row_of > k, work[:, k : k + 1] / pivot[:, k : k + 1], 0.0)
+            work = work - factor * pivot
+        diagonal = jnp.where(row_id == col_id, work[:, :block], 0.0)
+        norm = jnp.sqrt(jnp.sum(diagonal, axis=1, keepdims=True))
+        inverse = jnp.where(col_id <= row_id, work[:, block:] / norm, 0.0)
         exact = dict(precision=lax.Precision.HIGHEST, preferred_element_type=jnp.float32)
         coeffs = lax.dot_general(cross, inverse, NT, **exact)
         mixed = jnp.dot(coeffs, inverse, **exact)
@@ -256,18 +262,19 @@
 
     keep = jnp.where(band == 0, 0.0, 1.0).astype(jnp.float32)
     lhs = weights[...]
-    flat = o_ref.reshape(block * rows, NZ)
-
-    @pl.loop(0, rows // planes)
+
+    @pl.loop(0, rows // 8, unroll=2)
     def _(i):
-        base = i * planes
-        high, low = split(jnp.concatenate([b_ref[base + p] for p in range(planes)], axis=1))
+        base = pl.multiple_of(i * 8, 8)
+        cells = [base + p for p in range(8)]
+        high, low = split(jnp.concatenate([b_ref[cell] for cell in cells], axis=1))
         rhs = jnp.concatenate([high, high, low, low], axis=0)
         change = jnp.dot(lhs, rhs, preferred_element_type=jnp.float32)
-        for p in range(planes):
-            flat[pl.ds(base + p, block, stride=rows), :] = (
-                keep * a_ref[base + p] - change[:, p * NZ : (p + 1) * NZ]
-            )
+        fresh = [
+            keep * a_ref[cell] - change[:, p * NZ : (p + 1) * NZ]
+            for p, cell in enumerate(cells)
+        ]
+        o_ref[:, pl.ds(base, 8), :] = jnp.swapaxes(jnp.stack(fresh), 0, 1)
 
 
 def body(orbitals, potential):
@@ -285,20 +292,21 @@
     applied, basis, gram = pl.pallas_call(
         functools.partial(apply_kernel, nb, nd, planes, ny),
         out_shape=(cells, cells, jax.ShapeDtypeStruct((2 * block, NZ), jnp.float32)),
-        in_specs=[hbm, pl.BlockSpec(memory_space=pltpu.VMEM)],
+        in_specs=[hbm, hbm],
         out_specs=(hbm, hbm, hbm),
         scratch_shapes=[
             pltpu.VMEM((block, rows, NZ), jnp.float32),
             cells_vmem, cells_vmem, cells_vmem, cells_vmem, cells_vmem,
+            pltpu.VMEM((rows, NZ), jnp.float32),
             pltpu.VMEM((4 * block, 2 * block), jnp.float32),
             pltpu.VMEM((2 * block, NZ), jnp.float32),
             pltpu.VMEM((nd, 2 * block, NZ), jnp.float32),
             dma((chunk_count,)), dma((2, chunk_count)), dma((2, chunk_count)),
             dma((chunk_count,)), dma((chunk_count,)), dma((chunk_count,)), dma((chunk_count,)),
-            dma((nd,)), dma((nd,)), dma,
+            dma((nd,)), dma((nd,)), dma, dma,
         ],
         compiler_params=pltpu.CompilerParams(
-            collective_id=0, has_side_effects=True, vmem_limit_bytes=48 * MIB
+            collective_id=0, has_side_effects=True, vmem_limit_bytes=60 * MIB
         ),
         cost_estimate=pl.CostEstimate(
             flops=80 * block * rows * NZ, bytes_accessed=12 * block * rows * NZ, transcendentals=0
@@ -315,7 +323,7 @@
         in_specs=[pl.BlockSpec((2 * block, NZ), lambda i: (0, 0)), cell_spec, cell_spec],
         out_specs=pl.BlockSpec((block, step_rows, NZ), lambda i: (0, i, 0)),
         scratch_shapes=[pltpu.VMEM((block, 4 * block), jnp.bfloat16)],
-        compiler_params=pltpu.CompilerParams(vmem_limit_bytes=56 * MIB),
+        compiler_params=pltpu.CompilerParams(vmem_limit_bytes=60 * MIB),
         cost_estimate=pl.CostEstimate(
             flops=80 * block * rows * NZ, bytes_accessed=12 * block * rows * NZ, transcendentals=0
         ),

time: 197 us -> 184 us (0.934)
  Pallas kernels: 194 us -> 183 us
    pallas_call x1, Pallas kernels: 22.6 us -> 15.9 us  [body(): pl.pallas_call(functools.partial(finish_kernel, count, planes), grid=(row...]
    pallas_call x1, Pallas kernels: 171 us -> 167 us  [body(): pl.pallas_call(functools.partial(apply_kernel, nb, nd, planes, ny), out_s...]
where the time goes in v2:
time: 184 us; the launch traced here: 183 us
  Pallas kernels  183 us (99%)
    pallas_call x1, Pallas kernels, body(): pl.pallas_call(functools.partial(apply_kernel, nb, nd, planes, ny), out_s...  167 us
    pallas_call x1, Pallas kernels, body(): pl.pallas_call(functools.partial(finish_kernel, count, planes), grid=(row...  15.9 us

profile of v2, /device:TPU:31, one launch (start us, length us, event | category | flops | bytes accessed | tf_op | source)
XLA Modules:
  0.0 182.5 jit_solution(13399266029748675817)
XLA Ops:
  0.0 166.6 %apply_and_share.1 = (f32[384,32,128]{2,1,0:T(8,128)}, f32[384,32,128]{2,1,0:T(8,128)}, f32[64,128]{1,0:T(8,128)}) custom-call(f32[32,384,128]{2,1,0:T(8,128)} %bitcast.15, f32[384,128]{1,0:T(8,128)} %bitcast.16), custom_call_target="tpu_custom_call" | custom-call | flops 125829120 | bytes 18874368 | tf_op jit(solution)/shard_map/apply_and_share/pallas_call | solution.py:292
  166.6 15.9 %finish.1 = f32[32,384,128]{2,1,0:T(8,128)} custom-call(f32[64,128]{1,0:T(8,128)} %get-tuple-element.8.g_ref, f32[384,32,128]{2,1,0:T(8,128)} %get-tuple-element.9.a_ref, f32[384,32,128]{2,1,0:T(8,128)} %get-tuple-element.10.b_ref), custom_call_target="tpu_custom_call" | custom-call | flops 125829120 | bytes 18874368 | tf_op jit(solution)/shard_map/finish/pallas_call | solution.py:319

commit v3 on v2

--- a/solution.py
+++ b/solution.py
@@ -12,7 +12,7 @@
 COEFFS = (-205.0 / 72.0, 8.0 / 5.0, -1.0 / 5.0, 8.0 / 315.0, -1.0 / 560.0)
 HALF = tuple(-0.5 * c for c in COEFFS)
 CHUNK_Y = 2
-WINDOW = 8
+WINDOW = 4
 MIB = 1024 * 1024
 NT = (((1,), (1,)), ((), ()))
 MESH = pl.DeviceIdType.MESH
@@ -84,7 +84,20 @@
             recv_sem=part_recv.at[peer], device_id=(band, peer), device_id_type=MESH,
         )
 
-    @pl.loop(0, chunks)
+    wrapped = -(-WIDTH // CHUNK_Y)
+
+    def prepare(c):
+        load(c).wait()
+
+        @pl.loop(0, chunk // 8)
+        def _(i):
+            span = pl.ds(pl.multiple_of(c * chunk + i * 8, 8), 8)
+            xs[span] = jnp.swapaxes(nat[:, span, :], 0, 1)
+
+    for c in range(chunks - wrapped, chunks):
+        load(c).start()
+
+    @pl.loop(0, chunks - wrapped)
     def _(c):
         load(c).start()
 
@@ -104,22 +117,15 @@
     pl.semaphore_wait(barrier, nd + 1)
 
     acc[...] = jnp.zeros_like(acc)
-    flat = nat.reshape(block * rows, NZ)
-
-    @pl.loop(0, chunks)
+
+    @pl.loop(0, WINDOW)
     def _(c):
-        load(c).wait()
-
-        @pl.loop(0, chunk)
-        def _(i):
-            row = c * chunk + i
-            xs[row] = flat[pl.ds(row, block, stride=rows), :]
-
-        @pl.when(c < WINDOW)
-        def _():
-            halo(c, 0).start()
-            halo(c, 1).start()
-
+        prepare(c)
+        halo(c, 0).start()
+        halo(c, 1).start()
+
+    for c in range(chunks - wrapped, chunks):
+        prepare(c)
     potential.wait()
 
     def hamiltonian(c):
@@ -173,11 +179,6 @@
     def _(step):
         @pl.when(step < chunks)
         def _():
-            @pl.when(step + WINDOW < chunks)
-            def _():
-                halo(step + WINDOW, 0).start()
-                halo(step + WINDOW, 1).start()
-
             halo(step, 0).wait_recv()
             halo(step, 1).wait_recv()
             hamiltonian(step)
@@ -197,6 +198,17 @@
             save(c, 0).start()
             save(c, 1).start()
             gram(c)
+
+        ahead = step + WINDOW
+
+        @pl.when(ahead < chunks - wrapped)
+        def _():
+            prepare(ahead)
+
+        @pl.when(ahead < chunks)
+        def _():
+            halo(ahead, 0).start()
+            halo(ahead, 1).start()
 
     found = acc[...]
     found = found[: 2 * block] + found[2 * block :]
@@ -313,7 +325,7 @@
         ),
         name="apply_and_share",
     )(x, v)
-    step_rows = 8 * planes
+    step_rows = 16 * planes
     count = rows * NZ * nd
     cell_spec = pl.BlockSpec((step_rows, block, NZ), lambda i: (i, 0, 0))
     result = pl.pallas_call(

time: 184 us -> 177 us (0.962)
  Pallas kernels: 183 us -> 177 us
    pallas_call x1, Pallas kernels: 167 us -> 164 us  [body(): pl.pallas_call(functools.partial(apply_kernel, nb, nd, planes, ny), out_s...]
    pallas_call x1, Pallas kernels: 15.9 us -> 13.6 us  [body(): pl.pallas_call(functools.partial(finish_kernel, count, planes), grid=(row...]
where the time goes in v3:
time: 177 us
  Pallas kernels  177 us (100%)
    pallas_call x1, Pallas kernels, body(): pl.pallas_call(functools.partial(apply_kernel, nb, nd, planes, ny), out_s...  164 us
    pallas_call x1, Pallas kernels, body(): pl.pallas_call(functools.partial(finish_kernel, count, planes), grid=(row...  13.6 us

profile of v3, /device:TPU:31, one launch (start us, length us, event | category | flops | bytes accessed | tf_op | source)
XLA Modules:
  0.0 177.2 jit_solution(1901976855561320155)
XLA Ops:
  0.0 163.6 %apply_and_share.1 = (f32[384,32,128]{2,1,0:T(8,128)}, f32[384,32,128]{2,1,0:T(8,128)}, f32[64,128]{1,0:T(8,128)}) custom-call(f32[32,384,128]{2,1,0:T(8,128)} %bitcast.15, f32[384,128]{1,0:T(8,128)} %bitcast.16), custom_call_target="tpu_custom_call" | custom-call | flops 125829120 | bytes 18874368 | tf_op jit(solution)/shard_map/apply_and_share/pallas_call | solution.py:304
  163.6 13.6 %finish.1 = f32[32,384,128]{2,1,0:T(8,128)} custom-call(f32[64,128]{1,0:T(8,128)} %get-tuple-element.8.g_ref, f32[384,32,128]{2,1,0:T(8,128)} %get-tuple-element.9.a_ref, f32[384,32,128]{2,1,0:T(8,128)} %get-tuple-element.10.b_ref), custom_call_target="tpu_custom_call" | custom-call | flops 125829120 | bytes 18874368 | tf_op jit(solution)/shard_map/finish/pallas_call | solution.py:331

commit v4 on v3

--- a/solution.py
+++ b/solution.py
@@ -275,7 +275,7 @@
     keep = jnp.where(band == 0, 0.0, 1.0).astype(jnp.float32)
     lhs = weights[...]
 
-    @pl.loop(0, rows // 8, unroll=2)
+    @pl.loop(0, rows // 8, unroll=4)
     def _(i):
         base = pl.multiple_of(i * 8, 8)
         cells = [base + p for p in range(8)]
@@ -325,7 +325,7 @@
         ),
         name="apply_and_share",
     )(x, v)
-    step_rows = 16 * planes
+    step_rows = 24 * planes
     count = rows * NZ * nd
     cell_spec = pl.BlockSpec((step_rows, block, NZ), lambda i: (i, 0, 0))
     result = pl.pallas_call(

time: 177 us -> 176 us (level)
  no operation moved by 1% of the time
where the time goes in v4:
time: 176 us
  Pallas kernels  176 us (100%)
    pallas_call x1, Pallas kernels, body(): pl.pallas_call(functools.partial(apply_kernel, nb, nd, planes, ny), out_s...  164 us
    pallas_call x1, Pallas kernels, body(): pl.pallas_call(functools.partial(finish_kernel, count, planes), grid=(row...  12.1 us

profile of v4, /device:TPU:31, one launch (start us, length us, event | category | flops | bytes accessed | tf_op | source)
XLA Modules:
  0.0 175.7 jit_solution(11708462788956675344)
XLA Ops:
  0.0 163.6 %apply_and_share.1 = (f32[384,32,128]{2,1,0:T(8,128)}, f32[384,32,128]{2,1,0:T(8,128)}, f32[64,128]{1,0:T(8,128)}) custom-call(f32[32,384,128]{2,1,0:T(8,128)} %bitcast.15, f32[384,128]{1,0:T(8,128)} %bitcast.16), custom_call_target="tpu_custom_call" | custom-call | flops 125829120 | bytes 18874368 | tf_op jit(solution)/shard_map/apply_and_share/pallas_call | solution.py:304
  163.6 12.1 %finish.1 = f32[32,384,128]{2,1,0:T(8,128)} custom-call(f32[64,128]{1,0:T(8,128)} %get-tuple-element.8.g_ref, f32[384,32,128]{2,1,0:T(8,128)} %get-tuple-element.9.a_ref, f32[384,32,128]{2,1,0:T(8,128)} %get-tuple-element.10.b_ref), custom_call_target="tpu_custom_call" | custom-call | flops 125829120 | bytes 18874368 | tf_op jit(solution)/shard_map/finish/pallas_call | solution.py:331
